TPU v7x, 32 devices: a whole 2x2x4 slice. The times are simulated.
32 devices in a mesh: blk: 8 (over z, x), dp: 4 (over y, core).
Axes of the slice: x: 2, y: 2, z: 4, core: 2. Of those that a mesh axis runs over, the one named last changes fastest.
Arguments:
- audio_frames: bfloat16 [4, 512, 16, 1024], P('dp', 'blk'), may hold values from -6 to 6
- conv_weight: bfloat16 [3072, 1024], replicated, may hold values from -0.109375 to 0.109375
- proj_weight: bfloat16 [1024, 512], replicated, may hold values from -0.1875 to 0.1875
- text_embed: bfloat16 [4, 512, 512], P('dp', 'blk'), may hold values from -6 to 6
- pair_langs: int32 [4, 512], P('dp', 'blk'), may hold values from 0 to 99, as said below
- log_scale: float32 [100], replicated, may hold values from 2 to 5
- lang_bias: float32 [100], replicated, may hold values from 95 to 105
- log_var: float32 [100], replicated, may hold values from -1 to 1
Outputs:
- loss: float32 [], replicated
- scale_grad: float32 [100], replicated
- var_grad: float32 [100], replicated
- conv_grad: float32 [3072, 1024], P('blk', 'dp')
- proj_grad: float32 [1024, 512], P('blk', 'dp')
- text_grad: float32 [4, 512, 512], P('dp', 'blk')
Inputs may be any that keep to these rules, and one draw needn't show every extreme that they name: `pair_langs`: language ids of the pairs; in every draw some languages are named by no pair.
All inputs are finite; a program needn't handle non-finite values.
Results may differ from a plain program's by a relative error of at most 0.029.
Values may be sent and summed in bfloat16 or wider, within the bound.
A program may use at most 128 MiB of HBM per device.

v0:
```python
import jax
import jax.numpy as jnp
from jax import lax
from jax.sharding import PartitionSpec as P

epsilon = 1e-06


def stack_taps(frames):
    clips, steps_count, channels = frames.shape
    blank = jnp.zeros_like(frames[:, :1])
    before = jnp.concatenate([blank, frames[:, :-1]], axis=1)
    after = jnp.concatenate([frames[:, 1:], blank], axis=1)
    return jnp.concatenate([before, frames, after], axis=2).reshape(
        clips * steps_count, 3 * channels
    )


def encode(frames, conv_weight, proj_weight):
    clips, steps_count, channels = frames.shape
    stacked = stack_taps(frames)
    preact = jnp.dot(stacked, conv_weight, preferred_element_type=jnp.float32)
    pooled = jnp.mean(jax.nn.gelu(preact).reshape(clips, steps_count, -1), axis=1).astype(
        jnp.bfloat16
    )
    embedding = jnp.dot(pooled, proj_weight, preferred_element_type=jnp.float32)
    audio_len = jnp.sqrt(jnp.sum(embedding * embedding, axis=-1, keepdims=True) + epsilon)
    return (stacked, preact, pooled, embedding / audio_len, audio_len)


def normalize_text(text_rows):
    text_float = text_rows.astype(jnp.float32)
    text_len = jnp.sqrt(jnp.sum(text_float * text_float, axis=-1, keepdims=True) + epsilon)
    return (text_float / text_len, text_len)


def encode_back(stacked, preact, pooled, audio_unit, audio_len, grad_audio, proj_weight):
    clips = pooled.shape[0]
    steps_count = preact.shape[0] // clips
    radial = jnp.sum(audio_unit * grad_audio, axis=-1, keepdims=True)
    grad_embed = ((grad_audio - audio_unit * radial) / audio_len).astype(jnp.bfloat16)
    proj_term = lax.dot_general(
        pooled, grad_embed, (((0,), (0,)), ((), ())), preferred_element_type=jnp.float32
    )
    grad_pooled = (
        lax.dot_general(
            grad_embed, proj_weight, (((1,), (1,)), ((), ())), preferred_element_type=jnp.float32
        )
        / steps_count
    )
    grad_act = jnp.broadcast_to(
        grad_pooled[:, None, :], (clips, steps_count, grad_pooled.shape[1])
    ).reshape(clips * steps_count, -1)
    grad_pre = jax.vjp(jax.nn.gelu, preact)[1](grad_act)[0].astype(jnp.bfloat16)
    conv_term = lax.dot_general(
        stacked, grad_pre, (((0,), (0,)), ((), ())), preferred_element_type=jnp.float32
    )
    return (conv_term, proj_term)


def local(
    audio_frames, conv_weight, proj_weight, text_embed, pair_langs, log_scale, lang_bias, log_var
):
    frames = audio_frames[0]
    text_rows = text_embed[0]
    pair_ids = pair_langs[0]
    local_pairs = frames.shape[0]
    classes = jnp.arange(log_scale.shape[0], dtype=jnp.int32)
    onehot = (pair_ids[:, None] == classes[None, :]).astype(jnp.float32)
    counts = lax.psum(jnp.sum(onehot, axis=0), ("blk", "dp"))
    weight_table = jnp.exp(-log_var) / jnp.maximum(counts, 1.0)
    scale_table = jnp.exp(log_scale)
    stacked, preact, pooled, audio_unit, audio_len = encode(frames, conv_weight, proj_weight)
    audio_bf = audio_unit.astype(jnp.bfloat16)
    text_unit, text_len = normalize_text(text_rows)
    text_bf = text_unit.astype(jnp.bfloat16)
    all_text = lax.all_gather(text_bf, "blk", axis=0, tiled=True)
    all_ids = lax.all_gather(pair_ids, "blk", axis=0, tiled=True)
    pair_scale = jnp.sum(onehot * scale_table[None, :], axis=1)
    pair_bias = jnp.sum(onehot * lang_bias[None, :], axis=1)
    own_weight = jnp.sum(onehot * weight_table[None, :], axis=1)
    all_onehot = (all_ids[:, None] == classes[None, :]).astype(jnp.float32)
    col_weight = jnp.sum(all_onehot * weight_table[None, :], axis=1)
    logits = (
        pair_scale[:, None]
        * lax.dot_general(
            audio_bf, all_text, (((1,), (1,)), ((), ())), preferred_element_type=jnp.float32
        )
        + pair_bias[:, None]
    )
    row_max = jnp.max(logits, axis=1)
    row_lse = row_max + jnp.log(jnp.sum(jnp.exp(logits - row_max[:, None]), axis=1))
    local_max = jnp.max(logits, axis=0)
    joint_max = lax.pmax(local_max, "blk")
    joint_sum = lax.psum(jnp.sum(jnp.exp(logits - joint_max[None, :]), axis=0), "blk")
    col_lse = joint_max + jnp.log(joint_sum)
    offset = lax.axis_index("blk") * local_pairs
    own_cols = lax.dynamic_slice_in_dim(logits, offset, local_pairs, 1)
    positive = jnp.diagonal(own_cols)
    own_col_lse = lax.dynamic_slice_in_dim(col_lse, offset, local_pairs, 0)
    pair_loss = 0.5 * (row_lse + own_col_lse) - positive
    local_index = jnp.arange(local_pairs, dtype=jnp.int32)
    all_index = jnp.arange(logits.shape[1], dtype=jnp.int32)
    on_diagonal = all_index[None, :] == (offset + local_index)[:, None]
    score_grad = 0.5 * (
        own_weight[:, None] * jnp.exp(logits - row_lse[:, None])
        + col_weight[None, :] * jnp.exp(logits - col_lse[None, :])
    )
    score_grad = score_grad - jnp.where(on_diagonal, own_weight[:, None], 0.0)
    scale_terms = jnp.sum(score_grad * (logits - pair_bias[:, None]), axis=1)
    weighted = (score_grad * pair_scale[:, None]).astype(jnp.bfloat16)
    grad_audio = jnp.dot(weighted, all_text, preferred_element_type=jnp.float32)
    grad_text = lax.psum_scatter(
        lax.dot_general(
            weighted, audio_bf, (((0,), (0,)), ((), ())), preferred_element_type=jnp.float32
        ).astype(jnp.bfloat16),
        "blk",
        scatter_dimension=0,
        tiled=True,
    ).astype(jnp.float32)
    text_grad = (
        grad_text - text_unit * jnp.sum(text_unit * grad_text, axis=1, keepdims=True)
    ) / text_len
    conv_term, proj_term = encode_back(
        stacked, preact, pooled, audio_unit, audio_len, grad_audio, proj_weight
    )
    loss_sum, scale_grad = lax.psum(
        (
            jnp.sum(onehot * pair_loss[:, None], axis=0),
            jnp.sum(onehot * scale_terms[:, None], axis=0),
        ),
        ("blk", "dp"),
    )
    conv_half, proj_half = (
        lax.psum_scatter(
            conv_term.astype(jnp.bfloat16), "dp", scatter_dimension=1, tiled=True
        ).astype(jnp.float32),
        lax.psum_scatter(
            proj_term.astype(jnp.bfloat16), "dp", scatter_dimension=1, tiled=True
        ).astype(jnp.float32),
    )
    conv_grad, proj_grad = (
        lax.psum_scatter(
            conv_half.astype(jnp.bfloat16), "blk", scatter_dimension=0, tiled=True
        ).astype(jnp.float32),
        lax.psum_scatter(
            proj_half.astype(jnp.bfloat16), "blk", scatter_dimension=0, tiled=True
        ).astype(jnp.float32),
    )
    var_weight = jnp.exp(-log_var)
    lang_mean = loss_sum / jnp.maximum(counts, 1.0)
    loss = jnp.sum(var_weight * lang_mean + log_var)
    var_grad = 1.0 - var_weight * lang_mean
    return (loss, scale_grad, var_grad, conv_grad, proj_grad, text_grad[None])


def solution(mesh):
    return jax.shard_map(
        local,
        mesh=mesh,
        in_specs=(
            P("dp", "blk", None, None),
            P(),
            P(),
            P("dp", "blk", None),
            P("dp", "blk"),
            P(),
            P(),
            P(),
        ),
        out_specs=(P(), P(), P(), P("blk", "dp"), P("blk", "dp"), P("dp", "blk", None)),
        check_vma=False,
    )
```

profile of v0, /device:TPU:0, one launch (start us, length us, event | category | flops | bytes accessed | tf_op | source)
XLA Modules:
  0.0 453.0 jit_solution(11342273187059536071)
XLA Ops:
  7.2 3.3 fusion.26
  12.2 3.3 copy-done.21
  15.6 9.4 %bitcast_reduce_fusion = (f32[64,1024]{1,0:T(8,128)S(1)}, f32[1024,1024]{1,0:T(8,128)}) fusion(bf16[3072,1024]{1,0:T(8,128)(2,1)S(1)} %copy-done.21, bf16[1024,1024]{1,0:T(8,128)(2,1)S(1)} %bitcast.50, bf16[1024,1024]{1,0:T(8,128)(2,1)S(1)} %bitcast.45, bf16[1024,1024]{1,0:T(8,128)(2,1)S(1)} %bitcast.48), kind=kOutput, calls=%fused_computation.17 | convolution fusion | flops 6470696960 | bytes 17039360 | tf_op jit(solution)/shard_map/dot_general | solution.py:22
  26.1 42.0 %psum.30 = f32[100]{0:T(128)S(1)} all-reduce(f32[100]{0:T(128)S(1)} %convert_reduce_fusion), channel_id=1, replica_groups=mesh['blk'=8,'dp'=4] {'blk','dp'}, use_global_device_ids=true, to_apply=%region_14.0 | all-reduce | flops 100 | bytes 800 | tf_op jit(solution)/shard_map/psum | solution.py:70
  68.4 31.5 %all_gather.6 = bf16[512,512]{1,0:T(8,128)(2,1)S(1)} all-gather(bf16[64,512]{1,0:T(8,128)(2,1)S(1)} %fusion.23), channel_id=1, replica_groups=mesh['blk'=8,'dp'=4] {'blk'}, dimensions={0}, use_global_device_ids=true | all-gather | bytes 589824 | tf_op jit(solution)/shard_map/all_gather | solution.py:77
  100.8 2.0 fusion.25
  102.8 21.1 %pmax.7 = f32[512]{0:T(512)S(1)} all-reduce(f32[512]{0:T(512)S(1)} %get-tuple-element.8), channel_id=1, replica_groups=mesh['blk'=8,'dp'=4] {'blk'}, use_global_device_ids=true, to_apply=%region_8.0 | all-reduce | flops 512 | bytes 4096 | tf_op jit(solution)/shard_map/pmax | solution.py:94
  125.0 17.1 %psum.28 = f32[512]{0:T(512)S(1)} all-reduce(f32[512]{0:T(512)S(1)} %get-tuple-element.6), channel_id=1, replica_groups=mesh['blk'=8,'dp'=4] {'blk'}, use_global_device_ids=true, to_apply=%region_10.0 | all-reduce | flops 512 | bytes 4096 | tf_op jit(solution)/shard_map/psum | solution.py:95
  144.3 8.6 %all-reduce.2 = s32[512]{0:T(512)S(1)} all-reduce(s32[512]{0:T(512)S(1)} %bitcast_dynamic-update-slice_fusion), channel_id=2, replica_groups=mesh['blk'=8,'dp'=4] {'blk'}, use_global_device_ids=true, to_apply=%add.2 | all-reduce | flops 512 | bytes 4096
  153.9 1.6 multiply_reduce_fusion
  156.1 2.4 convolution_convert_fusion.1
  158.5 2.3 copy.14
  161.1 1.6 convolution_multiply_fusion
  162.7 4.4 fusion.6
  167.1 10.4 %convolution_convert_fusion = bf16[3072,1024]{1,0:T(8,128)(2,1)} fusion(bf16[1024,1024]{1,0:T(8,128)(2,1)S(1)} %fusion.6, bf16[1024,1024]{1,0:T(8,128)(2,1)S(1)} %bitcast.51, bf16[1024,1024]{1,0:T(8,128)(2,1)S(1)} %bitcast.46, bf16[1024,1024]{1,0:T(8,128)(2,1)S(1)} %bitcast.49), kind=kOutput, calls=%fused_computation.6 | convolution fusion | flops 6464471040 | bytes 14680064 | tf_op jit(solution)/shard_map/dot_general | solution.py:55
  179.9 6.5 %reduce-scatter.16.cloned.1.call-done = bf16[128,1024]{1,0:T(8,128)(2,1)} async-done(((bf16[512,1024]{1,0:T(8,128)(2,1)}), bf16[128,1024]{1,0:T(8,128)(2,1)}) %reduce-scatter.16.cloned.1.call-update) | async-done | bytes 262160
  186.4 1.8 copy.15
  188.2 59.2 %reduce-scatter.8.cloned.1.call-done = bf16[3072,256]{1,0:T(8,128)(2,1)} async-done(((bf16[3072,1024]{1,0:T(8,128)(2,1)}), bf16[3072,256]{1,0:T(8,128)(2,1)}) %reduce-scatter.8.cloned.1.call-update) | async-done | bytes 1572880 | tf_op jit(solution)/shard_map/reduce_scatter | solution.py:135
  247.8 39.5 %all-reduce.3 = (f32[100]{0:T(128)S(1)}, f32[100]{0:T(128)}) all-reduce(f32[100]{0:T(128)S(1)} %get-tuple-element.11, f32[100]{0:T(128)S(1)} %get-tuple-element.10), channel_id=1, replica_groups=mesh['blk'=8,'dp'=4] {'blk','dp'}, use_global_device_ids=true, to_apply=%region_12.0 | all-reduce | flops 200 | bytes 1600 | tf_op jit(solution)/shard_map/psum | solution.py:127
  288.5 24.3 %reduce-scatter.14.cloned.1.call-done = bf16[64,512]{1,0:T(8,128)(2,1)} async-done(((bf16[512,512]{1,0:T(8,128)(2,1)}), bf16[64,512]{1,0:T(8,128)(2,1)}) %reduce-scatter.14.cloned.1.call-update) | async-done | bytes 65552 | tf_op jit(solution)/shard_map/reduce_scatter | solution.py:113
  313.8 1.6 fusion.14
  315.4 61.8 %reduce-scatter.12.cloned.1.call-done = bf16[128,128]{1,0:T(8,128)(2,1)} async-done(((bf16[1024,128]{1,0:T(8,128)(2,1)}), bf16[128,128]{1,0:T(8,128)(2,1)}) %reduce-scatter.12.cloned.1.call-update) | async-done | bytes 32784 | tf_op jit(solution)/shard_map/reduce_scatter | solution.py:146
  378.6 66.2 %reduce-scatter.10.cloned.1.call-done = bf16[384,256]{1,0:T(8,128)(2,1)} async-done(((bf16[3072,256]{1,0:T(8,128)(2,1)}), bf16[384,256]{1,0:T(8,128)(2,1)}) %reduce-scatter.10.cloned.1.call-update) | async-done | bytes 196624 | tf_op jit(solution)/shard_map/reduce_scatter | solution.py:143
  444.7 1.7 convert_element_type.60
  (86 shorter events, 14.6 us)
Async XLA Ops:
  7.2 17.8 %copy-start = (bf16[1024,512]{1,0:T(8,128)(2,1)S(1)}, bf16[1024,512]{1,0:T(8,128)(2,1)}, u32[]{:S(2)}) copy-start(bf16[1024,512]{1,0:T(8,128)(2,1)} %param.10) | copy-start | bytes 3145732
  7.2 179.2 %reduce-scatter.16.cloned.1.call-start = ((), (), s32[]{:S(2)}) async-start(), calls=%async_computation.9 | async-start | bytes 1310720
  10.6 1.6 copy-start.1
  10.6 4.9 %copy-start.21 = (bf16[3072,1024]{1,0:T(8,128)(2,1)S(1)}, bf16[3072,1024]{1,0:T(8,128)(2,1)}, u32[]{:S(2)}) copy-start(bf16[3072,1024]{1,0:T(8,128)(2,1)} %param.9) | copy-start | bytes 18874372
  11.5 13.5 %copy-start.2 = (bf16[64,16,1024]{2,1,0:T(8,128)(2,1)}, bf16[64,16,1024]{2,1,0:T(8,128)(2,1)S(1)}, u32[]{:S(2)}) copy-start(bf16[64,16,1024]{2,1,0:T(8,128)(2,1)S(1)} %concatenate.20) | copy-start | bytes 6291460
  11.9 13.0 %copy-start.4 = (bf16[64,16,1024]{2,1,0:T(8,128)(2,1)}, bf16[64,16,1024]{2,1,0:T(8,128)(2,1)S(1)}, u32[]{:S(2)}) copy-start(bf16[64,16,1024]{2,1,0:T(8,128)(2,1)S(1)} %concatenate.23) | copy-start | bytes 6291460
  15.5 10.5 %copy-start.11 = (s32[1,64]{1,0:T(1,128)S(1)}, s32[1,64]{1,0:T(1,128)}, u32[]{:S(2)}) copy-start(s32[1,64]{1,0:T(1,128)} %param.12) | copy-start | bytes 772
  15.5 52.6 %copy-start.22 = (f32[100]{0:T(128)S(1)}, f32[100]{0:T(128)}, u32[]{:S(2)}) copy-start(f32[100]{0:T(128)} %param.13) | copy-start | bytes 1204
  15.5 52.6 %copy-start.6 = (bf16[1,64,512]{2,1,0:T(8,128)(2,1)S(1)}, bf16[1,64,512]{2,1,0:T(8,128)(2,1)}, u32[]{:S(2)}) copy-start(bf16[1,64,512]{2,1,0:T(8,128)(2,1)} %param.11) | copy-start | bytes 196612
  15.5 84.4 %copy-start.15 = (f32[100]{0:T(128)S(1)}, f32[100]{0:T(128)}, u32[]{:S(2)}) copy-start(f32[100]{0:T(128)} %param.15) | copy-start | bytes 1204
  15.5 84.4 %copy-start.14 = (f32[100]{0:T(128)S(1)}, f32[100]{0:T(128)}, u32[]{:S(2)}) copy-start(f32[100]{0:T(128)} %param.14) | copy-start | bytes 1204
  15.6 127.4 %copy-start.23 = (u32[32]{0:T(128)S(1)}, u32[32]{0:T(128)}, u32[]{:S(2)}) copy-start(u32[32]{0:T(128)} %constant.72) | copy-start | bytes 388
  26.0 76.7 %copy-start.12 = (f32[64]{0:T(128)}, f32[64]{0:T(128)S(1)}, u32[]{:S(2)}) copy-start(f32[64]{0:T(128)S(1)} %add_sqrt_fusion.1) | copy-start | bytes 772
  68.2 32.0 %copy-start.17 = (f32[100]{0:T(128)}, f32[100]{0:T(128)S(1)}, u32[]{:S(2)}) copy-start(f32[100]{0:T(128)S(1)} %psum.30) | copy-start | bytes 1204
  100.2 23.7 %copy-start.19 = (f32[64]{0:T(128)}, f32[64]{0:T(128)S(1)}, u32[]{:S(2)}) copy-start(f32[64]{0:T(128)S(1)} %get-tuple-element.14) | copy-start | bytes 772
  153.0 8.1 %copy-start.13 = (f32[64]{0:T(128)S(1)}, f32[64]{0:T(128)}, u32[]{:S(2)}) copy-start(f32[64]{0:T(128)} %copy-done.12) | copy-start | bytes 772
  160.9 86.6 %reduce-scatter.8.cloned.1.call-start = ((), (), s32[]{:S(2)}) async-start(), calls=%async_computation.5 | async-start | bytes 7864320 | tf_op jit(solution)/shard_map/reduce_scatter | solution.py:135
  161.1 6.0 %copy-start.3 = (bf16[64,16,1024]{2,1,0:T(8,128)(2,1)S(1)}, bf16[64,16,1024]{2,1,0:T(8,128)(2,1)}, u32[]{:S(2)}) copy-start(bf16[64,16,1024]{2,1,0:T(8,128)(2,1)} %copy-done.2) | copy-start | bytes 6291460
  161.1 6.0 %copy-start.5 = (bf16[64,16,1024]{2,1,0:T(8,128)(2,1)S(1)}, bf16[64,16,1024]{2,1,0:T(8,128)(2,1)}, u32[]{:S(2)}) copy-start(bf16[64,16,1024]{2,1,0:T(8,128)(2,1)} %copy-done.4) | copy-start | bytes 6291460
  177.6 109.8 %copy-start.16 = (f32[100]{0:T(128)S(1)}, f32[100]{0:T(128)}, u32[]{:S(2)}) copy-start(f32[100]{0:T(128)} %param.15) | copy-start | bytes 1204
  177.6 109.8 %copy-start.18 = (f32[100]{0:T(128)S(1)}, f32[100]{0:T(128)}, u32[]{:S(2)}) copy-start(f32[100]{0:T(128)} %copy-done.17) | copy-start | bytes 1204
  177.6 135.2 %reduce-scatter.14.cloned.1.call-start = ((), (), s32[]{:S(2)}) async-start(), calls=%async_computation.8 | async-start | bytes 589824 | tf_op jit(solution)/shard_map/reduce_scatter | solution.py:113
  179.8 197.4 %reduce-scatter.12.cloned.1.call-start = ((), (), s32[]{:S(2)}) async-start(), calls=%async_computation.7 | async-start | bytes 294912 | tf_op jit(solution)/shard_map/reduce_scatter | solution.py:146
  188.2 256.6 %reduce-scatter.10.cloned.1.call-start = ((), (), s32[]{:S(2)}) async-start(), calls=%async_computation.6 | async-start | bytes 1769472 | tf_op jit(solution)/shard_map/reduce_scatter | solution.py:143
  (5 other events, 4.3 us)
Sparse Core Ops, SparseCore 0:
  161.0 25.3 reduce-scatter.15
  189.1 58.3 reduce-scatter.7
  250.8 61.9 reduce-scatter.13
  316.9 60.2 reduce-scatter.11
  380.8 63.8 reduce-scatter.9
where the time goes:
time: 454 us; the launch traced here: 453 us
  waiting for transfers between devices  218 us (48%)
  blocking collectives  160 us (35%)
  matrix products  29.6 us (7%)
  local copies, waits for them, and re-layouts  16.9 us (4%)
  between operations  14.7 us (3%)
  other arithmetic  13.4 us (3%)
    reduce_scatter x1, waiting for transfers between devices, local(): lax.psum_scatter(conv_half.astype(jnp.bfloat16), 'blk', scatter_dimension...  66.2 us
    reduce_scatter x1, waiting for transfers between devices, local(): lax.psum_scatter(proj_half.astype(jnp.bfloat16), 'blk', scatter_dimension...  61.8 us
    reduce_scatter x1, waiting for transfers between devices, local(): lax.psum_scatter(conv_term.astype(jnp.bfloat16), 'dp', scatter_dimension=...  59.2 us
    psum x1, blocking collectives, local(): counts = lax.psum(jnp.sum(onehot, axis=0), ('blk', 'dp'))  42 us
    psum x1, blocking collectives, local(): lax.psum((jnp.sum(onehot * pair_loss[:, None], axis=0), jnp.sum(onehot *...  39.5 us
    all_gather x1, blocking collectives, local(): all_text = lax.all_gather(text_bf, 'blk', axis=0, tiled=True)  31.5 us
    reduce_scatter x1, waiting for transfers between devices, local(): lax.psum_scatter(lax.dot_general(weighted, audio_bf, (((0,), (0,)), ((),...  24.3 us
    pmax x1, blocking collectives, local(): joint_max = lax.pmax(local_max, 'blk')  21.1 us
  transfers between devices with their start and end apart: 5, of which 5 were waited for; matrix products, arithmetic and copies ran while one was open for 6% of the time, Pallas kernels for 0%

commit v1 on v0

v1 whole, which is shorter than its diff:
```python
import functools

import jax
import jax.numpy as jnp
from jax import lax
from jax.experimental import pallas as pl
from jax.experimental.pallas import tpu as pltpu
from jax.sharding import PartitionSpec as P

MESH = pl.DeviceIdType.MESH
F32 = jnp.float32
BF16 = jnp.bfloat16
epsilon = 1e-06
LANES = 128
VMEM_BYTES = 58 * 1024 * 1024


def dot(a, b, dims=((1,), (0,))):
    return lax.dot_general(a, b, (dims, ((), ())), preferred_element_type=F32)


def copy_to(src, dst, sends, recvs, index, device):
    return pltpu.make_async_remote_copy(
        src_ref=src,
        dst_ref=dst,
        send_sem=sends.at[index],
        recv_sem=recvs.at[index],
        device_id=device,
        device_id_type=MESH,
    )


def exchange(axis, count, part, sends, recvs):
    me = lax.axis_index(axis)
    return [
        copy_to(part(me), part(me), sends, recvs, o, {axis: lax.rem(me + o, count)})
        for o in range(1, count)
    ]


def greet(n_blk, n_dp):
    barrier = pltpu.get_barrier_semaphore()
    blk, dp = lax.axis_index("blk"), lax.axis_index("dp")
    for o in range(1, n_blk):
        pl.semaphore_signal(
            barrier, inc=1, device_id={"blk": lax.rem(blk + o, n_blk)}, device_id_type=MESH
        )
    for o in range(1, n_dp):
        pl.semaphore_signal(
            barrier, inc=1, device_id={"dp": lax.rem(dp + o, n_dp)}, device_id_type=MESH
        )
    pl.semaphore_wait(barrier, n_blk + n_dp - 2)


def shift_down(values, frame, steps):
    return jnp.where(frame == 0, 0.0, pltpu.roll(values, 1, 0))


def shift_up(values, frame, steps):
    return jnp.where(frame == steps - 1, 0.0, pltpu.roll(values, values.shape[0] - 1, 0))


def step_kernel(
    n_blk, n_dp, steps,
    frames, conv_w, proj_w, text, ids_col, ids_row, tables,
    pre_out, pooled, embed_out, text_term, sums_out,
    all_text, slope, ids_slots, count_slots, stat_slots,
    text_s, text_r, ids_s, ids_r, count_s, count_r, stat_s, stat_r,
):
    rows, cin = frames.shape
    width = conv_w.shape[1]
    clips = rows // steps
    group = ids_row.shape[1]
    blk, dp = lax.axis_index("blk"), lax.axis_index("dp")
    own = pl.ds(pl.multiple_of(blk * clips, clips), clips)

    ids_slots[blk] = ids_row[...]
    text_float = text[...].astype(F32)
    text_len = jnp.sqrt(jnp.sum(text_float * text_float, axis=1, keepdims=True) + epsilon)
    all_text[own, :] = (text_float / text_len).astype(BF16)
    greet(n_blk, n_dp)
    ids_copies = exchange("blk", n_blk, lambda b: ids_slots.at[b], ids_s, ids_r)
    text_copies = exchange(
        "blk", n_blk,
        lambda b: all_text.at[pl.ds(pl.multiple_of(b * clips, clips), clips), :],
        text_s, text_r,
    )
    for copy in ids_copies + text_copies:
        copy.start()

    tile = 256
    frame = lax.broadcasted_iota(jnp.int32, (rows, tile), 0) % steps
    c0, c1 = 0.7978845608028654, 0.044715

    @pl.loop(0, width // tile)
    def _(t):
        cols = pl.ds(pl.multiple_of(t * tile, tile), tile)
        x = dot(frames[...], conv_w[pl.ds(cin, cin), cols])
        x = x + shift_down(dot(frames[...], conv_w[pl.ds(0, cin), cols]), frame, steps)
        x = x + shift_up(dot(frames[...], conv_w[pl.ds(2 * cin, cin), cols]), frame, steps)
        square = x * x
        bend = jnp.tanh(c0 * x * (1.0 + c1 * square))
        half = 0.5 * (1.0 + bend)
        slope[:, cols] = half + 0.5 * x * (1.0 - bend * bend) * (c0 * (1.0 + 3.0 * c1 * square))
        act = (x * half).reshape(clips, steps, tile)
        pooled[:, cols] = (jnp.sum(act, axis=1) * (1.0 / steps)).astype(BF16)

    for copy in ids_copies:
        copy.wait()
    all_ids = ids_slots[0]
    for b in range(1, n_blk):
        all_ids = all_ids + ids_slots[b]
    across = (lax.broadcasted_iota(jnp.int32, (LANES, group), 0) == all_ids).astype(F32)
    eye = (
        lax.broadcasted_iota(jnp.int32, (LANES, LANES), 0)
        == lax.broadcasted_iota(jnp.int32, (LANES, LANES), 1)
    )
    batch_counts = jnp.sum(
        jnp.where(eye, jnp.sum(across, axis=1, keepdims=True), 0.0), axis=0, keepdims=True
    )
    count_slots[dp] = batch_counts
    count_copies = exchange("dp", n_dp, lambda d: count_slots.at[d], count_s, count_r)
    for copy in count_copies:
        copy.start()

    embedding = dot(pooled[...], proj_w[...])
    audio_len = jnp.sqrt(jnp.sum(embedding * embedding, axis=1, keepdims=True) + epsilon)
    audio_unit = embedding / audio_len
    audio_bf = audio_unit.astype(BF16)

    onehot = (lax.broadcasted_iota(jnp.int32, (clips, LANES), 1) == ids_col[...]).astype(F32)
    log_scale, bias, log_var = tables[0:1, :], tables[1:2, :], tables[2:3, :]
    pair_scale = jnp.sum(onehot * jnp.exp(log_scale), axis=1, keepdims=True)
    pair_bias = jnp.sum(onehot * bias, axis=1, keepdims=True)

    for copy in text_copies:
        copy.wait()
    logits = pair_scale * dot(audio_bf, all_text[...], ((1,), (1,))) + pair_bias
    local_max = jnp.max(logits, axis=0, keepdims=True)
    stat_slots[blk, 0:1, :] = local_max
    stat_slots[blk, 1:2, :] = jnp.sum(jnp.exp(logits - local_max), axis=0, keepdims=True)
    stat_copies = exchange("blk", n_blk, lambda b: stat_slots.at[b], stat_s, stat_r)
    for copy in stat_copies:
        copy.start()

    for copy in count_copies:
        copy.wait()
    counts = count_slots[0]
    for d in range(1, n_dp):
        counts = counts + count_slots[d]
    weight_row = jnp.exp(-log_var) / jnp.maximum(counts, 1.0)
    weight_col = jnp.sum(jnp.where(eye, weight_row, 0.0), axis=1, keepdims=True)
    own_weight = jnp.sum(onehot * weight_row, axis=1, keepdims=True)
    col_weight = jnp.sum(across * weight_col, axis=0, keepdims=True)
    row_max = jnp.max(logits, axis=1, keepdims=True)
    row_lse = row_max + jnp.log(jnp.sum(jnp.exp(logits - row_max), axis=1, keepdims=True))
    diagonal = (
        lax.broadcasted_iota(jnp.int32, (clips, group), 1)
        == lax.broadcasted_iota(jnp.int32, (clips, group), 0) + blk * clips
    )
    row_part = own_weight * jnp.exp(logits - row_lse)

    for copy in stat_copies:
        copy.wait()
    joint_max = stat_slots[0, 0:1, :]
    for b in range(1, n_blk):
        joint_max = jnp.maximum(joint_max, stat_slots[b, 0:1, :])
    joint_sum = jnp.zeros_like(joint_max)
    for b in range(n_blk):
        joint_sum = joint_sum + stat_slots[b, 1:2, :] * jnp.exp(
            stat_slots[b, 0:1, :] - joint_max
        )
    col_lse = joint_max + jnp.log(joint_sum)
    score = 0.5 * (row_part + col_weight * jnp.exp(logits - col_lse))
    score = score - jnp.where(diagonal, own_weight, 0.0)
    weighted = (score * pair_scale).astype(BF16)
    grad_audio = dot(weighted, all_text[...])
    radial = jnp.sum(audio_unit * grad_audio, axis=1, keepdims=True)
    grad_embed = ((grad_audio - audio_unit * radial) / audio_len).astype(BF16)
    embed_out[...] = grad_embed
    grad_pooled = dot(grad_embed, proj_w[...], ((1,), (1,))) * (1.0 / steps)
    text_term[...] = dot(weighted, audio_bf, ((0,), (0,))).astype(BF16)

    positive = jnp.sum(jnp.where(diagonal, logits, 0.0), axis=1, keepdims=True)
    own_col = jnp.sum(jnp.where(diagonal, col_lse, 0.0), axis=1, keepdims=True)
    pair_loss = 0.5 * (row_lse + own_col) - positive
    scale_terms = jnp.sum(score * (logits - pair_bias), axis=1, keepdims=True)
    sums_out[0:1, :] = jnp.sum(onehot * pair_loss, axis=0, keepdims=True)
    sums_out[1:2, :] = jnp.sum(onehot * scale_terms, axis=0, keepdims=True)
    sums_out[2:3, :] = counts

    for t in range(width // tile):
        cols = slice(t * tile, (t + 1) * tile)
        spread = jnp.broadcast_to(grad_pooled[:, None, cols], (clips, steps, tile))
        pre = spread.reshape(rows, tile) * slope[:, cols]
        pre_out[1, :, cols] = pre.astype(BF16)
        pre_out[0, :, cols] = shift_up(pre, frame, steps).astype(BF16)
        pre_out[2, :, cols] = shift_down(pre, frame, steps).astype(BF16)


def whole(count):
    return [pl.BlockSpec(memory_space=pltpu.VMEM)] * count


def forward_step(n_blk, n_dp, frames3, conv_weight, proj_weight, text_rows, pair_ids, tables):
    clips, steps, cin = frames3.shape
    rows, width, emb = clips * steps, conv_weight.shape[1], proj_weight.shape[1]
    group = clips * n_blk
    blk = lax.axis_index("blk")
    ids_row = jnp.where(
        jnp.arange(group, dtype=jnp.int32) // clips == blk, jnp.tile(pair_ids, n_blk), 0
    )[None, :]
    dma = pltpu.SemaphoreType.DMA
    return pl.pallas_call(
        functools.partial(step_kernel, n_blk, n_dp, steps),
        out_shape=(
            jax.ShapeDtypeStruct((3, rows, width), BF16),
            jax.ShapeDtypeStruct((clips, width), BF16),
            jax.ShapeDtypeStruct((clips, emb), BF16),
            jax.ShapeDtypeStruct((group, emb), BF16),
            jax.ShapeDtypeStruct((3, LANES), F32),
        ),
        in_specs=whole(7),
        out_specs=tuple(whole(5)),
        scratch_shapes=[
            pltpu.VMEM((group, emb), BF16),
            pltpu.VMEM((rows, width), F32),
            pltpu.VMEM((n_blk, 1, group), jnp.int32),
            pltpu.VMEM((n_dp, 1, LANES), F32),
            pltpu.VMEM((n_blk, 2, group), F32),
            dma((n_blk,)), dma((n_blk,)), dma((n_blk,)), dma((n_blk,)),
            dma((n_dp,)), dma((n_dp,)), dma((n_blk,)), dma((n_blk,)),
        ],
        compiler_params=pltpu.CompilerParams(
            collective_id=0, has_side_effects=True, vmem_limit_bytes=VMEM_BYTES
        ),
        cost_estimate=pl.CostEstimate(
            flops=6 * rows * cin * width, bytes_accessed=20 * 2**20, transcendentals=rows * width
        ),
    )(
        frames3.reshape(rows, cin), conv_weight, proj_weight, text_rows,
        pair_ids[:, None], ids_row, tables,
    )


def reduce_plain(frames, pre, pooled, grad_embed, text_term, sums):
    conv_term = jnp.concatenate(
        [dot(frames, pre[tap], ((0,), (0,))).astype(BF16) for tap in range(3)], axis=0
    )
    proj_term = dot(pooled, grad_embed, ((0,), (0,))).astype(BF16)
    grad_text = lax.psum_scatter(text_term, "blk", scatter_dimension=0, tiled=True).astype(F32)
    totals = lax.psum(sums[:2], ("blk", "dp"))

    def scatter(term):
        half = lax.psum_scatter(term, "dp", scatter_dimension=1, tiled=True)
        return lax.psum_scatter(half, "blk", scatter_dimension=0, tiled=True).astype(F32)

    return scatter(conv_term), scatter(proj_term), grad_text, totals


def local(
    n_blk, n_dp,
    audio_frames, conv_weight, proj_weight, text_embed, pair_langs, log_scale, lang_bias, log_var,
):
    langs = log_scale.shape[0]
    frames3, text_rows, pair_ids = audio_frames[0], text_embed[0], pair_langs[0]
    tables = jnp.pad(jnp.stack([log_scale, lang_bias, log_var]), ((0, 0), (0, LANES - langs)))
    pre, pooled, grad_embed, text_term, sums = forward_step(
        n_blk, n_dp, frames3, conv_weight, proj_weight, text_rows, pair_ids, tables
    )
    frames = frames3.reshape(-1, frames3.shape[2])
    reduce = reduce_plain
    conv_grad, proj_grad, grad_text, totals = reduce(
        frames, pre, pooled, grad_embed, text_term, sums
    )
    text_float = text_rows.astype(F32)
    text_len = jnp.sqrt(jnp.sum(text_float * text_float, axis=-1, keepdims=True) + epsilon)
    text_unit = text_float / text_len
    text_grad = (
        grad_text - text_unit * jnp.sum(text_unit * grad_text, axis=1, keepdims=True)
    ) / text_len
    loss_sum, scale_grad = totals[0, :langs], totals[1, :langs]
    counts = sums[2, :langs]
    var_weight = jnp.exp(-log_var)
    lang_mean = loss_sum / jnp.maximum(counts, 1.0)
    loss = jnp.sum(var_weight * lang_mean + log_var)
    var_grad = 1.0 - var_weight * lang_mean
    return (loss, scale_grad, var_grad, conv_grad, proj_grad, text_grad[None])


def solution(mesh):
    return jax.shard_map(
        functools.partial(local, mesh.shape["blk"], mesh.shape["dp"]),
        mesh=mesh,
        in_specs=(
            P("dp", "blk", None, None),
            P(),
            P(),
            P("dp", "blk", None),
            P("dp", "blk"),
            P(),
            P(),
            P(),
        ),
        out_specs=(P(), P(), P(), P("blk", "dp"), P("blk", "dp"), P("dp", "blk", None)),
        check_vma=False,
    )
```

time: 454 us -> 337 us (0.74)
  blocking collectives: 160 us -> 39.5 us
  Pallas kernels: 0 us -> 33.7 us
  matrix products: 29.6 us -> 13.6 us
  local copies, waits for them, and re-layouts: 16.9 us -> 5.81 us
  waiting for transfers between devices: 218 us -> 208 us
  other arithmetic: 13.4 us -> 22 us
    psum x3 -> x1, blocking collectives: 98.7 us -> 39.5 us  [reduce_plain(): totals = lax.psum(sums[:2], ('blk', 'dp'))]
    pallas_call x0 -> x1, Pallas kernels: none -> 33.7 us  [forward_step(): pl.pallas_call(functools.partial(step_kernel, n_blk, n_dp, steps), out_sh...]
    all_gather x1 -> x0, blocking collectives: 31.5 us -> none  [local(): all_text = lax.all_gather(text_bf, 'blk', axis=0, tiled=True)]
    pmax x1 -> x0, blocking collectives: 21.1 us -> none  [local(): joint_max = lax.pmax(local_max, 'blk')]
    dot_general x8 -> x4, matrix products: 29.6 us -> 13.6 us  [dot(): return lax.dot_general(a, b, (dims, ((), ())), preferred_element_type=F32)]
    concatenate x1, other arithmetic: 0.01 us -> 13.1 us  [reduce_plain(): jnp.concatenate([dot(frames, pre[tap], ((0,), (0,))).astype(BF16) for tap...]
    unnamed x1 -> x0, blocking collectives: 8.58 us -> none
    unnamed x53 -> x10, local copies, waits for them, and re-layouts: 10.7 us -> 3.19 us
  transfers between devices with their start and end apart: 5 -> 5, of which waited for: 5 -> 4; matrix products, arithmetic and copies ran while one was open for 6% -> 10% of each run, Pallas kernels for 0% -> 0%
where the time goes in v1:
time: 337 us
  waiting for transfers between devices  208 us (62%)
  blocking collectives  39.5 us (12%)
  Pallas kernels  33.7 us (10%)
  other arithmetic  22 us (7%)
  between operations  13.9 us (4%)
  matrix products  13.6 us (4%)
  local copies, waits for them, and re-layouts  5.81 us (2%)
    reduce_scatter x2, waiting for transfers between devices, scatter(): lax.psum_scatter(half, 'blk', scatter_dimension=0, tiled=True).astype(F32)  128 us
    reduce_scatter x1, waiting for transfers between devices, scatter(): half = lax.psum_scatter(term, 'dp', scatter_dimension=1, tiled=True)  55.4 us
    psum x1, blocking collectives, reduce_plain(): totals = lax.psum(sums[:2], ('blk', 'dp'))  39.5 us
    pallas_call x1, Pallas kernels, forward_step(): pl.pallas_call(functools.partial(step_kernel, n_blk, n_dp, steps), out_sh...  33.7 us
    reduce_scatter x1, waiting for transfers between devices, reduce_plain(): lax.psum_scatter(text_term, 'blk', scatter_dimension=0, tiled=True)  24 us
    dot_general x4, matrix products, dot(): return lax.dot_general(a, b, (dims, ((), ())), preferred_element_type=F32)  13.6 us
    concatenate x1, other arithmetic, reduce_plain(): jnp.concatenate([dot(frames, pre[tap], ((0,), (0,))).astype(BF16) for tap...  13.1 us
  transfers between devices with their start and end apart: 5, of which 4 were waited for; matrix products, arithmetic and copies ran while one was open for 10% of the time, Pallas kernels for 0%

profile of v1, /device:TPU:0, one launch (start us, length us, event | category | flops | bytes accessed | tf_op | source)
XLA Modules:
  0.0 336.9 jit_solution(15096502430196875894)
XLA Ops:
  7.2 0.7 tile.11
  8.0 1.4 copy.15.ids_col
  9.3 0.6 compare_select_fusion.ids_row
  9.9 1.3 select_maximum_fusion.tables
  11.2 33.7 %shard_map.127 = (bf16[3,1024,1024]{2,1,0:T(8,128)(2,1)}, bf16[64,1024]{1,0:T(8,128)(2,1)}, bf16[64,512]{1,0:T(8,128)(2,1)}, bf16[512,512]{1,0:T(8,128)(2,1)}, f32[3,128]{1,0:T(4,128)}) custom-call(bf16[1024,1024]{1,0:T(8,128)(2,1)} %bitcast.53, bf16[3072,1024]{1,0:T(8,128)(2,1)} %conv_w.1, bf16[1024,512]{1,0:T(8,128)(2,1)} %proj_w.1, ...), custom_call_target="tpu_custom_call" | custom-call | flops 6442450944 | bytes 20971520 | tf_op jit(solution)/shard_map/pallas_call | solution.py:214
  44.9 1.5 convolution_convert_fusion
  46.4 1.4 copy.16
  48.1 4.0 %convert_bitcast_fusion = bf16[1024,1024]{1,0:T(8,128)(2,1)S(1)} fusion(bf16[1024,1024]{1,0:T(8,128)(2,1)S(1)} %bitcast.54, bf16[3,1024,1024]{2,1,0:T(8,128)(2,1)} %get-tuple-element.12), kind=kOutput, calls=%fused_computation.7 | convolution fusion | flops 2148532224 | bytes 6291456 | tf_op jit(solution)/shard_map/dot_general | solution.py:19
  52.0 4.1 %convert_bitcast_fusion.1 = bf16[1024,1024]{1,0:T(8,128)(2,1)S(1)} fusion(bf16[1024,1024]{1,0:T(8,128)(2,1)S(1)} %bitcast.55, bf16[3,1024,1024]{2,1,0:T(8,128)(2,1)} %get-tuple-element.12), kind=kOutput, calls=%fused_computation.9 | convolution fusion | flops 2148532224 | bytes 6291456 | tf_op jit(solution)/shard_map/dot_general | solution.py:19
  56.2 4.0 %convert_bitcast_fusion.2 = bf16[1024,1024]{1,0:T(8,128)(2,1)S(1)} fusion(bf16[1024,1024]{1,0:T(8,128)(2,1)S(1)} %bitcast.56, bf16[3,1024,1024]{2,1,0:T(8,128)(2,1)} %get-tuple-element.12), kind=kOutput, calls=%fused_computation.11 | convolution fusion | flops 2148532224 | bytes 6291456 | tf_op jit(solution)/shard_map/dot_general | solution.py:19
  60.1 13.1 %pad_maximum_fusion = bf16[3072,1024]{1,0:T(8,128)(2,1)} fusion(bf16[1024,1024]{1,0:T(8,128)(2,1)S(1)} %convert_bitcast_fusion, bf16[1024,1024]{1,0:T(8,128)(2,1)S(1)} %convert_bitcast_fusion.1, bf16[1024,1024]{1,0:T(8,128)(2,1)S(1)} %convert_bitcast_fusion.2), kind=kLoop, calls=%fused_computation | loop fusion | flops 18874368 | bytes 12582912 | tf_op jit(solution)/shard_map/concatenate | solution.py:247
  73.4 0.7 reduce-scatter.14.cloned.1.call-update
  74.2 1.8 copy.17
  76.0 55.4 %reduce-scatter.8.cloned.1.call-done = bf16[3072,256]{1,0:T(8,128)(2,1)} async-done(((bf16[3072,1024]{1,0:T(8,128)(2,1)}), bf16[3072,256]{1,0:T(8,128)(2,1)}) %reduce-scatter.8.cloned.1.call-update) | async-done | bytes 1572880 | tf_op jit(solution)/shard_map/reduce_scatter | solution.py:255
  131.5 39.5 %psum.7 = f32[2,128]{1,0:T(2,128)S(1)} all-reduce(f32[2,128]{1,0:T(2,128)S(1)} %slice.21), channel_id=1, replica_groups=mesh['blk'=8,'dp'=4] {'blk','dp'}, use_global_device_ids=true, to_apply=%region_0.1 | all-reduce | flops 256 | bytes 2048 | tf_op jit(solution)/shard_map/psum | solution.py:252
  171.0 0.5 broadcast_subtract_fusion
  171.6 0.6 add_reduce_fusion
  172.8 24.0 %reduce-scatter.14.cloned.1.call-done = bf16[64,512]{1,0:T(8,128)(2,1)} async-done(((bf16[512,512]{1,0:T(8,128)(2,1)}), bf16[64,512]{1,0:T(8,128)(2,1)}) %reduce-scatter.14.cloned.1.call-update) | async-done | bytes 65552 | tf_op jit(solution)/shard_map/reduce_scatter | solution.py:251
  196.8 1.0 fusion.15
  197.8 1.6 fusion.17
  199.4 61.7 %reduce-scatter.12.cloned.1.call-done = bf16[128,128]{1,0:T(8,128)(2,1)} async-done(((bf16[1024,128]{1,0:T(8,128)(2,1)}), bf16[128,128]{1,0:T(8,128)(2,1)}) %reduce-scatter.12.cloned.1.call-update) | async-done | bytes 32784 | tf_op jit(solution)/shard_map/reduce_scatter | solution.py:256
  261.1 1.4 convert_element_type.43
  262.5 66.2 %reduce-scatter.10.cloned.1.call-done = bf16[384,256]{1,0:T(8,128)(2,1)} async-done(((bf16[3072,256]{1,0:T(8,128)(2,1)}), bf16[384,256]{1,0:T(8,128)(2,1)}) %reduce-scatter.10.cloned.1.call-update) | async-done | bytes 196624 | tf_op jit(solution)/shard_map/reduce_scatter | solution.py:256
  328.7 1.7 convert_element_type.41
  (23 shorter events, 1.2 us)
Async XLA Ops:
  7.2 67.0 %reduce-scatter.16.cloned.1.call-start = ((), (), s32[]{:S(2)}) async-start(), calls=%async_computation.9 | async-start | bytes 1310720
  44.9 3.2 copy-start.3
  47.8 83.6 %reduce-scatter.8.cloned.1.call-start = ((), (), s32[]{:S(2)}) async-start(), calls=%async_computation.5 | async-start | bytes 7864320 | tf_op jit(solution)/shard_map/reduce_scatter | solution.py:255
  73.3 58.2 %copy-start.2 = (f32[3,128]{1,0:T(4,128)S(1)}, f32[3,128]{1,0:T(4,128)}, u32[]{:S(2)}) copy-start(f32[3,128]{1,0:T(4,128)} %get-tuple-element.11) | copy-start | bytes 4612
  73.3 97.7 %copy-start.1 = (f32[100]{0:T(128)S(1)}, f32[100]{0:T(128)}, u32[]{:S(2)}) copy-start(f32[100]{0:T(128)} %param.15) | copy-start | bytes 1204
  73.3 98.8 %copy-start = (bf16[1,64,512]{2,1,0:T(8,128)(2,1)S(1)}, bf16[1,64,512]{2,1,0:T(8,128)(2,1)}, u32[]{:S(2)}) copy-start(bf16[1,64,512]{2,1,0:T(8,128)(2,1)} %param.11) | copy-start | bytes 196612
  73.3 123.4 %reduce-scatter.14.cloned.1.call-start = ((), (), s32[]{:S(2)}) async-start(), calls=%async_computation.8 | async-start | bytes 589824 | tf_op jit(solution)/shard_map/reduce_scatter | solution.py:251
  74.1 187.1 %reduce-scatter.12.cloned.1.call-start = ((), (), s32[]{:S(2)}) async-start(), calls=%async_computation.7 | async-start | bytes 294912 | tf_op jit(solution)/shard_map/reduce_scatter | solution.py:256
  76.0 252.7 %reduce-scatter.10.cloned.1.call-start = ((), (), s32[]{:S(2)}) async-start(), calls=%async_computation.6 | async-start | bytes 1769472 | tf_op jit(solution)/shard_map/reduce_scatter | solution.py:256
Sparse Core Ops, SparseCore 0:
  47.9 22.3 reduce-scatter.15
  73.4 57.9 reduce-scatter.7
  134.8 61.9 reduce-scatter.13
  200.9 60.2 reduce-scatter.11
  264.8 63.8 reduce-scatter.9

commit v2 on v1

--- a/solution.py
+++ b/solution.py
@@ -243,6 +243,209 @@
     )
 
 
+def reduce_kernel(
+    steps,
+    frames_t, pre, pooled, grad_embed, text_term, sums,
+    conv_out, proj_out, text_out, totals_out,
+    parts, core_in, first_in, second_in, z_in, text_in, sum_in, total_in,
+    core_s, core_r, first_s, first_r, second_s, second_r, z_s, z_r,
+    text_s, text_r, sum_s, sum_r, total_s, total_r,
+):
+    n_z, n_blk, n_dp = steps, text_in.shape[0], total_in.shape[0]
+    blk, dp = lax.axis_index("blk"), lax.axis_index("dp")
+    z, x, y, core = blk // 2, blk % 2, dp // 2, dp % 2
+    clips = text_in.shape[1]
+    cin = frames_t.shape[0]
+    wide = conv_out.shape[1]
+    conv_rows = conv_out.shape[0]
+    proj_rows, proj_cols = proj_out.shape
+    half = proj_rows // 2
+    tile = 256
+    tiles = 2 * conv_rows // tile
+
+    text_in[blk] = text_term[pl.ds(pl.multiple_of(blk * clips, clips), clips), :]
+    sum_in[blk] = sums[0:2, :]
+    greet(n_blk, n_dp)
+    small = exchange("blk", n_blk, lambda b: sum_in.at[b], sum_s, sum_r)
+    for copy in small:
+        copy.start()
+
+    def compute(s):
+        target = lax.rem(z + 1 + s, n_z)
+        for m in range(tiles):
+            block = target * tiles + m
+            tap = block // (cin // tile)
+            channel = pl.ds(pl.multiple_of(lax.rem(block, cin // tile) * tile, tile), tile)
+            for d in range(n_dp):
+                cols = slice(d * wide, (d + 1) * wide)
+                term = dot(frames_t[channel, :], pre[tap, :, cols]).astype(BF16)
+                row = m * tile
+                while row < (m + 1) * tile:
+                    side = row // conv_rows
+                    stop = min((side + 1) * conv_rows, (m + 1) * tile)
+                    parts[(s, d % 2) + order(s, d // 2, side)
+                          + (slice(row - side * conv_rows, stop - side * conv_rows),)] = (
+                        term[row - m * tile : stop - m * tile]
+                    )
+                    row = stop
+        start = pl.multiple_of(target * 2 * proj_rows, 2 * proj_rows)
+        proj_term = dot(
+            pooled[:, pl.ds(start, 2 * proj_rows)], grad_embed[...], ((0,), (0,))
+        ).astype(BF16)
+        for d in range(n_dp):
+            for side in range(2):
+                for part in range(2):
+                    top = side * proj_rows + part * half
+                    parts[(s, d % 2) + order(s, d // 2, side)
+                          + (slice(conv_rows, conv_rows + half),
+                             slice(part * proj_cols, (part + 1) * proj_cols))] = (
+                        proj_term[top : top + half, d * proj_cols : (d + 1) * proj_cols]
+                    )
+
+    def order(s, along_y, along_x):
+        return (along_y, along_x) if s % 2 == 0 else (along_x, along_y)
+
+    y_peer = {"dp": dp + 2 - 4 * y}
+    x_peer = {"blk": blk + 1 - 2 * x}
+    core_peer = {"dp": dp + 1 - 2 * core}
+    core_copy, first_copy, second_copy, z_copy = [], [], [], []
+    for s in range(n_z):
+        first_at, second_at = order(s, y, x)
+        first_peer, second_peer = (y_peer, x_peer) if s % 2 == 0 else (x_peer, y_peer)
+        core_copy.append(
+            copy_to(parts.at[s, 1 - core], core_in.at[s], core_s, core_r, s, core_peer)
+        )
+        first_copy.append(
+            copy_to(
+                parts.at[s, core, 1 - first_at], first_in.at[s], first_s, first_r, s, first_peer
+            )
+        )
+        second_copy.append(
+            copy_to(
+                parts.at[s, core, first_at, 1 - second_at], second_in.at[s],
+                second_s, second_r, s, second_peer,
+            )
+        )
+        if s < n_z - 1:
+            target = lax.rem(z + 1 + s, n_z)
+            z_copy.append(
+                copy_to(
+                    parts.at[s, core, first_at, second_at], z_in.at[s], z_s, z_r, s,
+                    {"blk": target * 2 + x},
+                )
+            )
+
+    def add(ref, arrived):
+        ref[...] = (ref[...].astype(F32) + arrived[...].astype(F32)).astype(BF16)
+
+    text_copies, total_copies = [], []
+    for t in range(n_z + 3):
+        if t < n_z:
+            compute(t)
+            core_copy[t].start()
+        if 0 <= t - 1 < n_z:
+            s = t - 1
+            core_copy[s].wait()
+            add(parts.at[s, core], core_in.at[s])
+            first_copy[s].start()
+        if t == 1:
+            for o in range(1, n_blk):
+                peer = lax.rem(blk + o, n_blk)
+                text_copies.append(
+                    copy_to(
+                        text_term.at[pl.ds(pl.multiple_of(peer * clips, clips), clips), :],
+                        text_in.at[blk], text_s, text_r, o, {"blk": peer},
+                    )
+                )
+                text_copies[-1].start()
+            for copy in small:
+                copy.wait()
+            total = sum_in[0]
+            for b in range(1, n_blk):
+                total = total + sum_in[b]
+            total_in[dp] = total
+            total_copies = exchange("dp", n_dp, lambda d: total_in.at[d], total_s, total_r)
+            for copy in total_copies:
+                copy.start()
+        if 0 <= t - 2 < n_z:
+            s = t - 2
+            first_at, _ = order(s, y, x)
+            first_copy[s].wait()
+            add(parts.at[s, core, first_at], first_in.at[s])
+            second_copy[s].start()
+        if 0 <= t - 3 < n_z:
+            s = t - 3
+            first_at, second_at = order(s, y, x)
+            second_copy[s].wait()
+            if s < n_z - 1:
+                add(parts.at[s, core, first_at, second_at], second_in.at[s])
+                z_copy[s].start()
+
+    for copy in total_copies:
+        copy.wait()
+    total = total_in[0]
+    for d in range(1, n_dp):
+        total = total + total_in[d]
+    totals_out[...] = total
+    for copy in text_copies:
+        copy.wait()
+    grad_text = text_in[0].astype(F32)
+    for b in range(1, n_blk):
+        grad_text = grad_text + text_in[b].astype(F32)
+    text_out[...] = grad_text
+    for copy in z_copy:
+        copy.wait()
+    last = n_z - 1
+    first_at, second_at = order(last, y, x)
+    whole_sum = parts[last, core, first_at, second_at].astype(F32)
+    whole_sum = whole_sum + second_in[last].astype(F32)
+    for s in range(last):
+        whole_sum = whole_sum + z_in[s].astype(F32)
+    conv_out[...] = whole_sum[:conv_rows]
+    proj_out[:half, :] = whole_sum[conv_rows:, :proj_cols]
+    proj_out[half:, :] = whole_sum[conv_rows:, proj_cols:]
+
+
+def reduce_fused(n_blk, n_dp, frames, pre, pooled, grad_embed, text_term, sums):
+    rows, cin = frames.shape
+    width, (clips, emb) = pre.shape[2], grad_embed.shape
+    n_z = n_blk // 2
+    conv_rows, wide = 3 * cin // n_blk, width // n_dp
+    proj_rows, proj_cols = width // n_blk, emb // n_dp
+    height = conv_rows + proj_rows // 2
+    dma = pltpu.SemaphoreType.DMA
+    return pl.pallas_call(
+        functools.partial(reduce_kernel, n_z),
+        out_shape=(
+            jax.ShapeDtypeStruct((conv_rows, wide), F32),
+            jax.ShapeDtypeStruct((proj_rows, proj_cols), F32),
+            jax.ShapeDtypeStruct((clips, emb), F32),
+            jax.ShapeDtypeStruct((2, LANES), F32),
+        ),
+        in_specs=whole(6),
+        out_specs=tuple(whole(4)),
+        scratch_shapes=[
+            pltpu.VMEM((n_z, 2, 2, 2, height, wide), BF16),
+            pltpu.VMEM((n_z, 2, 2, height, wide), BF16),
+            pltpu.VMEM((n_z, 2, height, wide), BF16),
+            pltpu.VMEM((n_z, height, wide), BF16),
+            pltpu.VMEM((n_z, height, wide), BF16),
+            pltpu.VMEM((n_blk, clips, emb), BF16),
+            pltpu.VMEM((n_blk, 2, LANES), F32),
+            pltpu.VMEM((n_dp, 2, LANES), F32),
+        ]
+        + [dma((n_z,))] * 8
+        + [dma((n_blk,))] * 4
+        + [dma((n_dp,))] * 2,
+        compiler_params=pltpu.CompilerParams(
+            collective_id=1, has_side_effects=True, vmem_limit_bytes=VMEM_BYTES
+        ),
+        cost_estimate=pl.CostEstimate(
+            flops=6 * rows * cin * width, bytes_accessed=10 * 2**20, transcendentals=0
+        ),
+    )(frames.T, pre, pooled, grad_embed, text_term, sums)
+
+
 def reduce_plain(frames, pre, pooled, grad_embed, text_term, sums):
     conv_term = jnp.concatenate(
         [dot(frames, pre[tap], ((0,), (0,))).astype(BF16) for tap in range(3)], axis=0
@@ -269,7 +472,8 @@
         n_blk, n_dp, frames3, conv_weight, proj_weight, text_rows, pair_ids, tables
     )
     frames = frames3.reshape(-1, frames3.shape[2])
-    reduce = reduce_plain
+    boxed = n_dp == 4 and n_blk % 2 == 0 and conv_weight.shape[1] // n_dp == 2 * LANES
+    reduce = functools.partial(reduce_fused, n_blk, n_dp) if boxed else reduce_plain
     conv_grad, proj_grad, grad_text, totals = reduce(
         frames, pre, pooled, grad_embed, text_term, sums
     )

time: 337 us -> 108 us (0.32)
  waiting for transfers between devices: 208 us -> 0 us
  Pallas kernels: 33.7 us -> 91.7 us
  blocking collectives: 39.5 us -> 0 us
  other arithmetic: 22 us -> 6.56 us
  matrix products: 13.6 us -> 0 us
  between operations: 13.9 us -> 0.68 us
    reduce_scatter x4 -> x0, waiting for transfers between devices: 207 us -> none  [the longest x2 128 us: scatter(): lax.psum_scatter(half, 'blk', scatter_dimension=0, tiled=True).astype(F32)]
    pallas_call x0 -> x1, Pallas kernels: none -> 57.9 us  [reduce_fused(): pl.pallas_call(functools.partial(reduce_kernel, n_z), out_shape=(jax.Shap...]
    psum x1 -> x0, blocking collectives: 39.5 us -> none  [reduce_plain(): totals = lax.psum(sums[:2], ('blk', 'dp'))]
    dot_general x4 -> x0, matrix products: 13.6 us -> none  [dot(): return lax.dot_general(a, b, (dims, ((), ())), preferred_element_type=F32)]
    concatenate x1 -> x0, other arithmetic: 13.1 us -> none  [reduce_plain(): jnp.concatenate([dot(frames, pre[tap], ((0,), (0,))).astype(BF16) for tap...]
  transfers between devices with their start and end apart: 5 -> 0, of which waited for: 4 -> 0; matrix products, arithmetic and copies ran while one was open for 10% -> 0% of each run, Pallas kernels for 0% -> 0%
where the time goes in v2:
time: 108 us
  Pallas kernels  91.7 us (85%)
  local copies, waits for them, and re-layouts  9.11 us (8%)
  other arithmetic  6.56 us (6%)
    pallas_call x1, Pallas kernels, reduce_fused(): pl.pallas_call(functools.partial(reduce_kernel, n_z), out_shape=(jax.Shap...  57.9 us
    pallas_call x1, Pallas kernels, forward_step(): pl.pallas_call(functools.partial(step_kernel, n_blk, n_dp, steps), out_sh...  33.8 us
    unnamed x8, local copies, waits for them, and re-layouts  3.25 us
    another operation x1, local copies, waits for them, and re-layouts, local(): frames = frames3.reshape(-1, frames3.shape[2])  2.59 us

profile of v2, /device:TPU:0, one launch (start us, length us, event | category | flops | bytes accessed | tf_op | source)
XLA Modules:
  0.0 108.0 jit_solution(10894024631056578123)
XLA Ops:
  0.6 1.4 %copy.18.ids_col = s32[64,1]{1,0:T(8,128)} copy(s32[64,1]{0,1:T(1,128)} %bitcast.22) | data formatting | bytes 512 | tf_op jit(solution)/shard_map/broadcast_in_dim;squeeze | solution.py:242
  2.0 0.7 tile.11
  2.6 0.1 tile.12
  2.7 0.6 compare_select_fusion.ids_row
  3.3 1.3 %select_maximum_fusion.tables = f32[3,128]{1,0:T(4,128)} fusion(f32[1,100]{1,0:T(1,128)} %bitcast.24, f32[1,100]{1,0:T(1,128)} %bitcast.25, f32[1,100]{1,0:T(1,128)} %bitcast.26), kind=kLoop, calls=%fused_computation.10 | loop fusion | flops 2304 | bytes 2736 | tf_op jit(solution)/shard_map/stack | solution.py:470
  4.6 0.0 copy-start
  4.6 33.8 %shard_map.127 = (bf16[3,1024,1024]{2,1,0:T(8,128)(2,1)}, bf16[64,1024]{1,0:T(8,128)(2,1)}, bf16[64,512]{1,0:T(8,128)(2,1)}, bf16[512,512]{1,0:T(8,128)(2,1)}, f32[3,128]{1,0:T(4,128)}) custom-call(bf16[1024,1024]{1,0:T(8,128)(2,1)} %bitcast.18, bf16[3072,1024]{1,0:T(8,128)(2,1)} %conv_w.1, bf16[1024,512]{1,0:T(8,128)(2,1)} %proj_w.1, ...), custom_call_target="tpu_custom_call" | custom-call | flops 6442450944 | bytes 20971520 | tf_op jit(solution)/shard_map/pallas_call | solution.py:214
  38.4 0.0 copy-done
  38.4 2.6 %copy.17 = bf16[1024,1024]{0,1:T(8,128)(2,1)} copy(bf16[1024,1024]{1,0:T(8,128)(2,1)S(1)} %bitcast.19) | data formatting | bytes 4194304 | tf_op jit(solution)/shard_map/reshape;squeeze | solution.py:474
  41.0 0.0 copy-start.1
  41.0 0.0 copy-start.2
  41.0 57.9 %shard_map.128 = (f32[384,256]{1,0:T(8,128)}, f32[128,128]{1,0:T(8,128)}, f32[64,512]{1,0:T(8,128)}, f32[2,128]{1,0:T(2,128)}) custom-call(bf16[1024,1024]{1,0:T(8,128)(2,1)} %bitcast.20, bf16[3,1024,1024]{2,1,0:T(8,128)(2,1)} %get-tuple-element.15.pre, bf16[64,1024]{1,0:T(8,128)(2,1)} %get-tuple-element.16.pooled, ...), custom_call_target="tpu_custom_call" | custom-call | flops 6442450944 | bytes 10485760 | tf_op jit(solution)/shard_map/pallas_call | solution.py:417
  98.9 0.0 copy-done.1
  98.9 0.1 fusion
  99.0 1.1 %multiply_reduce_fusion = f32[64]{0:T(128)S(1)} fusion(f32[64,512]{1,0:T(8,128)} %get-tuple-element.23, f32[64]{0:T(128)S(1)} %add_sqrt_fusion, bf16[1,64,512]{2,1,0:T(8,128)(2,1)S(1)} %copy-done.1), kind=kLoop, calls=%fused_computation.4 | loop fusion | flops 131008 | bytes 197120 | tf_op jit(solution)/shard_map/reduce_sum | solution.py:484
  100.1 1.7 %divide_bitcast_fusion = f32[1,64,512]{2,1,0:T(8,128)} fusion(f32[64,512]{1,0:T(8,128)} %get-tuple-element.23, f32[64]{0:T(128)S(1)} %multiply_reduce_fusion, f32[64]{0:T(128)S(1)} %add_sqrt_fusion, bf16[1,64,512]{2,1,0:T(8,128)(2,1)S(1)} %copy-done.1), kind=kLoop, calls=%fused_computation.3 | loop fusion | flops 163840 | bytes 328192 | tf_op jit(solution)/shard_map/broadcast_in_dim | solution.py:492
  101.8 0.0 copy-done.2
  101.8 1.2 %broadcast_subtract_fusion = (f32[100]{0:T(128)}, f32[100]{0:T(128)S(1)}) fusion(f32[3,128]{1,0:T(4,128)} %get-tuple-element.19.sums, f32[2,128]{1,0:T(2,128)} %get-tuple-element.20, f32[100]{0:T(128)S(1)} %copy-done.2), kind=kLoop, calls=%fused_computation.18 | loop fusion | flops 500 | bytes 2000 | tf_op jit(solution)/shard_map/sub | solution.py:491
  103.0 0.6 add_reduce_fusion
  103.6 1.2 %slice_bitcast_fusion = f32[100]{0:T(128)} fusion(f32[2,128]{1,0:T(2,128)} %get-tuple-element.20), kind=kLoop, calls=%fused_computation.15 | loop fusion | bytes 800 | tf_op jit(solution)/shard_map/squeeze | solution.py:486
  104.8 1.8 %copy.21 = f32[384,256]{1,0:T(8,128)} copy(f32[384,256]{1,0:T(8,128)} %get-tuple-element.35) | data formatting | bytes 786432
  106.6 1.5 %copy.22 = f32[128,128]{1,0:T(8,128)} copy(f32[128,128]{1,0:T(8,128)} %get-tuple-element.36) | data formatting | bytes 131072
  (1 shorter events, 0.0 us)
Async XLA Ops:
  4.6 33.8 %copy-start = (bf16[1,64,16,1024]{3,2,1,0:T(8,128)(2,1)S(1)}, bf16[1,64,16,1024]{3,2,1,0:T(8,128)(2,1)}, u32[]{:S(2)}) copy-start(bf16[1,64,16,1024]{3,2,1,0:T(8,128)(2,1)} %param.8) | copy-start | bytes 6291460
  41.0 57.9 %copy-start.1 = (bf16[1,64,512]{2,1,0:T(8,128)(2,1)S(1)}, bf16[1,64,512]{2,1,0:T(8,128)(2,1)}, u32[]{:S(2)}) copy-start(bf16[1,64,512]{2,1,0:T(8,128)(2,1)} %param.11) | copy-start | bytes 196612
  41.0 60.8 %copy-start.2 = (f32[100]{0:T(128)S(1)}, f32[100]{0:T(128)}, u32[]{:S(2)}) copy-start(f32[100]{0:T(128)} %param.15) | copy-start | bytes 1204

commit v3 on v2

--- a/solution.py
+++ b/solution.py
@@ -62,19 +62,34 @@
 
 def step_kernel(
     n_blk, n_dp, steps,
-    frames, conv_w, proj_w, text, ids_col, ids_row, tables,
+    frames, conv_w, proj_w, text, ids, log_scale_in, bias_in, log_var_in,
     pre_out, pooled, embed_out, text_term, sums_out,
-    all_text, slope, ids_slots, count_slots, stat_slots,
+    all_text, slope, tables, ids_slots, count_slots, stat_slots,
     text_s, text_r, ids_s, ids_r, count_s, count_r, stat_s, stat_r,
+    frames_t=None,
 ):
     rows, cin = frames.shape
     width = conv_w.shape[1]
     clips = rows // steps
-    group = ids_row.shape[1]
+    group = all_text.shape[0]
+    langs = log_var_in.shape[1]
     blk, dp = lax.axis_index("blk"), lax.axis_index("dp")
     own = pl.ds(pl.multiple_of(blk * clips, clips), clips)
 
-    ids_slots[blk] = ids_row[...]
+    tables[...] = jnp.zeros_like(tables)
+    tables[0:1, :langs] = log_scale_in[...]
+    tables[1:2, :langs] = bias_in[...]
+    tables[2:3, :langs] = log_var_in[...]
+    diagonal = (
+        lax.broadcasted_iota(jnp.int32, (clips, group), 1)
+        == lax.broadcasted_iota(jnp.int32, (clips, group), 0) + blk * clips
+    )
+    same = (
+        lax.broadcasted_iota(jnp.int32, (clips, clips), 0)
+        == lax.broadcasted_iota(jnp.int32, (clips, clips), 1)
+    )
+    ids_col = jnp.sum(jnp.where(same, ids[...].astype(F32), 0.0), axis=1, keepdims=True)
+    ids_slots[blk] = jnp.sum(jnp.where(diagonal, ids_col, 0.0), axis=0, keepdims=True)
     text_float = text[...].astype(F32)
     text_len = jnp.sqrt(jnp.sum(text_float * text_float, axis=1, keepdims=True) + epsilon)
     all_text[own, :] = (text_float / text_len).astype(BF16)
@@ -110,7 +125,9 @@
     all_ids = ids_slots[0]
     for b in range(1, n_blk):
         all_ids = all_ids + ids_slots[b]
-    across = (lax.broadcasted_iota(jnp.int32, (LANES, group), 0) == all_ids).astype(F32)
+    across = (
+        lax.broadcasted_iota(jnp.int32, (LANES, group), 0) == all_ids.astype(jnp.int32)
+    ).astype(F32)
     eye = (
         lax.broadcasted_iota(jnp.int32, (LANES, LANES), 0)
         == lax.broadcasted_iota(jnp.int32, (LANES, LANES), 1)
@@ -128,7 +145,9 @@
     audio_unit = embedding / audio_len
     audio_bf = audio_unit.astype(BF16)
 
-    onehot = (lax.broadcasted_iota(jnp.int32, (clips, LANES), 1) == ids_col[...]).astype(F32)
+    onehot = (
+        lax.broadcasted_iota(jnp.int32, (clips, LANES), 1) == ids_col.astype(jnp.int32)
+    ).astype(F32)
     log_scale, bias, log_var = tables[0:1, :], tables[1:2, :], tables[2:3, :]
     pair_scale = jnp.sum(onehot * jnp.exp(log_scale), axis=1, keepdims=True)
     pair_bias = jnp.sum(onehot * bias, axis=1, keepdims=True)
@@ -154,11 +173,14 @@
     col_weight = jnp.sum(across * weight_col, axis=0, keepdims=True)
     row_max = jnp.max(logits, axis=1, keepdims=True)
     row_lse = row_max + jnp.log(jnp.sum(jnp.exp(logits - row_max), axis=1, keepdims=True))
-    diagonal = (
-        lax.broadcasted_iota(jnp.int32, (clips, group), 1)
-        == lax.broadcasted_iota(jnp.int32, (clips, group), 0) + blk * clips
-    )
     row_part = own_weight * jnp.exp(logits - row_lse)
+
+    if frames_t is not None:
+
+        @pl.loop(0, cin // tile)
+        def _(t):
+            cols = pl.ds(pl.multiple_of(t * tile, tile), tile)
+            frames_t[cols, :] = frames[:, cols].T
 
     for copy in stat_copies:
         copy.wait()
@@ -202,56 +224,61 @@
     return [pl.BlockSpec(memory_space=pltpu.VMEM)] * count
 
 
-def forward_step(n_blk, n_dp, frames3, conv_weight, proj_weight, text_rows, pair_ids, tables):
-    clips, steps, cin = frames3.shape
-    rows, width, emb = clips * steps, conv_weight.shape[1], proj_weight.shape[1]
+def step_shapes(n_blk, clips, steps, width, emb):
+    return (
+        ((3, clips * steps, width), BF16),
+        ((clips, width), BF16),
+        ((clips, emb), BF16),
+        ((clips * n_blk, emb), BF16),
+        ((3, LANES), F32),
+    )
+
+
+def step_scratch(n_blk, n_dp, clips, steps, width, emb):
     group = clips * n_blk
-    blk = lax.axis_index("blk")
-    ids_row = jnp.where(
-        jnp.arange(group, dtype=jnp.int32) // clips == blk, jnp.tile(pair_ids, n_blk), 0
-    )[None, :]
     dma = pltpu.SemaphoreType.DMA
+    return [
+        pltpu.VMEM((group, emb), BF16),
+        pltpu.VMEM((clips * steps, width), F32),
+        pltpu.VMEM((8, LANES), F32),
+        pltpu.VMEM((n_blk, 1, group), F32),
+        pltpu.VMEM((n_dp, 1, LANES), F32),
+        pltpu.VMEM((n_blk, 2, group), F32),
+        dma((n_blk,)), dma((n_blk,)), dma((n_blk,)), dma((n_blk,)),
+        dma((n_dp,)), dma((n_dp,)), dma((n_blk,)), dma((n_blk,)),
+    ]
+
+
+def forward_step(n_blk, n_dp, steps, operands):
+    frames, conv_weight, proj_weight, text_rows = operands[:4]
+    (rows, cin), clips = frames.shape, text_rows.shape[0]
+    width, emb = proj_weight.shape
     return pl.pallas_call(
         functools.partial(step_kernel, n_blk, n_dp, steps),
-        out_shape=(
-            jax.ShapeDtypeStruct((3, rows, width), BF16),
-            jax.ShapeDtypeStruct((clips, width), BF16),
-            jax.ShapeDtypeStruct((clips, emb), BF16),
-            jax.ShapeDtypeStruct((group, emb), BF16),
-            jax.ShapeDtypeStruct((3, LANES), F32),
-        ),
-        in_specs=whole(7),
+        out_shape=tuple(
+            jax.ShapeDtypeStruct(*shape) for shape in step_shapes(n_blk, clips, steps, width, emb)
+        ),
+        in_specs=whole(8),
         out_specs=tuple(whole(5)),
-        scratch_shapes=[
-            pltpu.VMEM((group, emb), BF16),
-            pltpu.VMEM((rows, width), F32),
-            pltpu.VMEM((n_blk, 1, group), jnp.int32),
-            pltpu.VMEM((n_dp, 1, LANES), F32),
-            pltpu.VMEM((n_blk, 2, group), F32),
-            dma((n_blk,)), dma((n_blk,)), dma((n_blk,)), dma((n_blk,)),
-            dma((n_dp,)), dma((n_dp,)), dma((n_blk,)), dma((n_blk,)),
-        ],
+        scratch_shapes=step_scratch(n_blk, n_dp, clips, steps, width, emb),
         compiler_params=pltpu.CompilerParams(
             collective_id=0, has_side_effects=True, vmem_limit_bytes=VMEM_BYTES
         ),
         cost_estimate=pl.CostEstimate(
             flops=6 * rows * cin * width, bytes_accessed=20 * 2**20, transcendentals=rows * width
         ),
-    )(
-        frames3.reshape(rows, cin), conv_weight, proj_weight, text_rows,
-        pair_ids[:, None], ids_row, tables,
-    )
+    )(*operands)
 
 
 def reduce_kernel(
-    steps,
-    frames_t, pre, pooled, grad_embed, text_term, sums,
+    n_z,
+    frames_t, pre, pooled, grad_embed, text_term, sums, text, tables,
     conv_out, proj_out, text_out, totals_out,
     parts, core_in, first_in, second_in, z_in, text_in, sum_in, total_in,
     core_s, core_r, first_s, first_r, second_s, second_r, z_s, z_r,
     text_s, text_r, sum_s, sum_r, total_s, total_r,
 ):
-    n_z, n_blk, n_dp = steps, text_in.shape[0], total_in.shape[0]
+    n_blk, n_dp = text_in.shape[0], total_in.shape[0]
     blk, dp = lax.axis_index("blk"), lax.axis_index("dp")
     z, x, y, core = blk // 2, blk % 2, dp // 2, dp % 2
     clips = text_in.shape[1]
@@ -265,41 +292,42 @@
 
     text_in[blk] = text_term[pl.ds(pl.multiple_of(blk * clips, clips), clips), :]
     sum_in[blk] = sums[0:2, :]
-    greet(n_blk, n_dp)
     small = exchange("blk", n_blk, lambda b: sum_in.at[b], sum_s, sum_r)
     for copy in small:
         copy.start()
 
-    def compute(s):
+    def compute(s, which):
         target = lax.rem(z + 1 + s, n_z)
-        for m in range(tiles):
-            block = target * tiles + m
-            tap = block // (cin // tile)
-            channel = pl.ds(pl.multiple_of(lax.rem(block, cin // tile) * tile, tile), tile)
-            for d in range(n_dp):
-                cols = slice(d * wide, (d + 1) * wide)
+        start = pl.multiple_of(target * 2 * proj_rows, 2 * proj_rows)
+        for along_y in range(2):
+            d = along_y * 2 + which
+            cols = pl.ds(pl.multiple_of(d * wide, wide), wide)
+            for m in range(tiles):
+                block = target * tiles + m
+                tap = block // (cin // tile)
+                channel = pl.ds(pl.multiple_of(lax.rem(block, cin // tile) * tile, tile), tile)
                 term = dot(frames_t[channel, :], pre[tap, :, cols]).astype(BF16)
                 row = m * tile
                 while row < (m + 1) * tile:
                     side = row // conv_rows
                     stop = min((side + 1) * conv_rows, (m + 1) * tile)
-                    parts[(s, d % 2) + order(s, d // 2, side)
-                          + (slice(row - side * conv_rows, stop - side * conv_rows),)] = (
+                    at = (s, which) + order(s, along_y, side)
+                    parts[at + (slice(row - side * conv_rows, stop - side * conv_rows),)] = (
                         term[row - m * tile : stop - m * tile]
                     )
                     row = stop
-        start = pl.multiple_of(target * 2 * proj_rows, 2 * proj_rows)
-        proj_term = dot(
-            pooled[:, pl.ds(start, 2 * proj_rows)], grad_embed[...], ((0,), (0,))
-        ).astype(BF16)
-        for d in range(n_dp):
+            proj_term = dot(
+                pooled[:, pl.ds(start, 2 * proj_rows)],
+                grad_embed[:, pl.ds(pl.multiple_of(d * proj_cols, proj_cols), proj_cols)],
+                ((0,), (0,)),
+            ).astype(BF16)
             for side in range(2):
                 for part in range(2):
                     top = side * proj_rows + part * half
-                    parts[(s, d % 2) + order(s, d // 2, side)
-                          + (slice(conv_rows, conv_rows + half),
-                             slice(part * proj_cols, (part + 1) * proj_cols))] = (
-                        proj_term[top : top + half, d * proj_cols : (d + 1) * proj_cols]
+                    at = (s, which) + order(s, along_y, side)
+                    parts[at + (slice(conv_rows, conv_rows + half),
+                                slice(part * proj_cols, (part + 1) * proj_cols))] = (
+                        proj_term[top : top + half]
                     )
 
     def order(s, along_y, along_x):
@@ -341,8 +369,9 @@
     text_copies, total_copies = [], []
     for t in range(n_z + 3):
         if t < n_z:
-            compute(t)
+            compute(t, 1 - core)
             core_copy[t].start()
+            compute(t, core)
         if 0 <= t - 1 < n_z:
             s = t - 1
             core_copy[s].wait()
@@ -386,13 +415,23 @@
     total = total_in[0]
     for d in range(1, n_dp):
         total = total + total_in[d]
-    totals_out[...] = total
+    log_var = tables[2:3, :]
+    var_weight = jnp.exp(-log_var)
+    lang_mean = total[0:1, :] / jnp.maximum(sums[2:3, :], 1.0)
+    loss = jnp.sum(var_weight * lang_mean + log_var, axis=1, keepdims=True)
+    totals_out[0:1, :] = jnp.broadcast_to(loss, (1, LANES))
+    totals_out[1:2, :] = total[1:2, :]
+    totals_out[2:3, :] = 1.0 - var_weight * lang_mean
     for copy in text_copies:
         copy.wait()
     grad_text = text_in[0].astype(F32)
     for b in range(1, n_blk):
         grad_text = grad_text + text_in[b].astype(F32)
-    text_out[...] = grad_text
+    text_float = text[...].astype(F32)
+    text_len = jnp.sqrt(jnp.sum(text_float * text_float, axis=1, keepdims=True) + epsilon)
+    text_unit = text_float / text_len
+    radial = jnp.sum(text_unit * grad_text, axis=1, keepdims=True)
+    text_out[...] = (grad_text - text_unit * radial) / text_len
     for copy in z_copy:
         copy.wait()
     last = n_z - 1
@@ -406,25 +445,39 @@
     proj_out[half:, :] = whole_sum[conv_rows:, proj_cols:]
 
 
-def reduce_fused(n_blk, n_dp, frames, pre, pooled, grad_embed, text_term, sums):
-    rows, cin = frames.shape
-    width, (clips, emb) = pre.shape[2], grad_embed.shape
+def fused_kernel(n_blk, n_dp, steps, *refs):
+    operands, results, rest = refs[:8], refs[8:12], refs[12:]
+    kept, frames_t, rest = rest[:5], rest[5], rest[6:]
+    step_part, reduce_part = rest[:14], rest[14:]
+    step_kernel(n_blk, n_dp, steps, *operands, *kept, *step_part, frames_t=frames_t)
+    reduce_kernel(n_blk // 2, frames_t, *kept, operands[3], step_part[2], *results, *reduce_part)
+
+
+def fused_step(n_blk, n_dp, steps, operands):
+    frames, conv_weight, proj_weight, text_rows = operands[:4]
+    (rows, cin), clips = frames.shape, text_rows.shape[0]
+    width, emb = proj_weight.shape
     n_z = n_blk // 2
     conv_rows, wide = 3 * cin // n_blk, width // n_dp
     proj_rows, proj_cols = width // n_blk, emb // n_dp
     height = conv_rows + proj_rows // 2
     dma = pltpu.SemaphoreType.DMA
     return pl.pallas_call(
-        functools.partial(reduce_kernel, n_z),
+        functools.partial(fused_kernel, n_blk, n_dp, steps),
         out_shape=(
             jax.ShapeDtypeStruct((conv_rows, wide), F32),
             jax.ShapeDtypeStruct((proj_rows, proj_cols), F32),
             jax.ShapeDtypeStruct((clips, emb), F32),
-            jax.ShapeDtypeStruct((2, LANES), F32),
-        ),
-        in_specs=whole(6),
+            jax.ShapeDtypeStruct((3, LANES), F32),
+        ),
+        in_specs=whole(8),
         out_specs=tuple(whole(4)),
         scratch_shapes=[
+            pltpu.VMEM(*shape) for shape in step_shapes(n_blk, clips, steps, width, emb)
+        ]
+        + [pltpu.VMEM((cin, rows), BF16)]
+        + step_scratch(n_blk, n_dp, clips, steps, width, emb)
+        + [
             pltpu.VMEM((n_z, 2, 2, 2, height, wide), BF16),
             pltpu.VMEM((n_z, 2, 2, height, wide), BF16),
             pltpu.VMEM((n_z, 2, height, wide), BF16),
@@ -441,9 +494,9 @@
             collective_id=1, has_side_effects=True, vmem_limit_bytes=VMEM_BYTES
         ),
         cost_estimate=pl.CostEstimate(
-            flops=6 * rows * cin * width, bytes_accessed=10 * 2**20, transcendentals=0
-        ),
-    )(frames.T, pre, pooled, grad_embed, text_term, sums)
+            flops=12 * rows * cin * width, bytes_accessed=10 * 2**20, transcendentals=rows * width
+        ),
+    )(*operands)
 
 
 def reduce_plain(frames, pre, pooled, grad_embed, text_term, sums):
@@ -466,15 +519,19 @@
     audio_frames, conv_weight, proj_weight, text_embed, pair_langs, log_scale, lang_bias, log_var,
 ):
     langs = log_scale.shape[0]
-    frames3, text_rows, pair_ids = audio_frames[0], text_embed[0], pair_langs[0]
-    tables = jnp.pad(jnp.stack([log_scale, lang_bias, log_var]), ((0, 0), (0, LANES - langs)))
-    pre, pooled, grad_embed, text_term, sums = forward_step(
-        n_blk, n_dp, frames3, conv_weight, proj_weight, text_rows, pair_ids, tables
-    )
-    frames = frames3.reshape(-1, frames3.shape[2])
-    boxed = n_dp == 4 and n_blk % 2 == 0 and conv_weight.shape[1] // n_dp == 2 * LANES
-    reduce = functools.partial(reduce_fused, n_blk, n_dp) if boxed else reduce_plain
-    conv_grad, proj_grad, grad_text, totals = reduce(
+    steps, cin = audio_frames.shape[2:]
+    frames, text_rows = audio_frames[0].reshape(-1, cin), text_embed[0]
+    operands = (
+        frames, conv_weight, proj_weight, text_rows, pair_langs,
+        log_scale[None], lang_bias[None], log_var[None],
+    )
+    if n_dp == 4 and n_blk % 2 == 0 and conv_weight.shape[1] // n_dp == 2 * LANES:
+        conv_grad, proj_grad, text_grad, rows = fused_step(n_blk, n_dp, steps, operands)
+        return (
+            rows[0, 0], rows[1, :langs], rows[2, :langs], conv_grad, proj_grad, text_grad[None]
+        )
+    pre, pooled, grad_embed, text_term, sums = forward_step(n_blk, n_dp, steps, operands)
+    conv_grad, proj_grad, grad_text, totals = reduce_plain(
         frames, pre, pooled, grad_embed, text_term, sums
     )
     text_float = text_rows.astype(F32)

time: 108 us -> 89.1 us (0.82)
  Pallas kernels: 91.7 us -> 80.9 us
  other arithmetic: 6.56 us -> 0 us
  local copies, waits for them, and re-layouts: 9.11 us -> 7.25 us
    pallas_call x2 -> x1, Pallas kernels: 91.7 us -> 80.9 us  [fused_step(): pl.pallas_call(functools.partial(fused_kernel, n_blk, n_dp, steps), out_s...]
    another operation x4 -> x0, local copies, waits for them, and re-layouts: 4.68 us -> none  [the longest x1 2.59 us: local(): frames = frames3.reshape(-1, frames3.shape[2])]
    reduce_sum x3 -> x0, other arithmetic: 1.82 us -> none  [the longest x1 1.11 us: local(): jnp.sum(text_unit * grad_text, axis=1, keepdims=True)]
    broadcast_in_dim x1 -> x0, other arithmetic: 1.66 us -> none  [local(): return (loss, scale_grad, var_grad, conv_grad, proj_grad, text_grad[None])]
    unnamed x8 -> x3, local copies, waits for them, and re-layouts: 3.25 us -> 4.8 us
    another operation x1 -> x0, other arithmetic: 1.27 us -> none  [local(): jnp.stack([log_scale, lang_bias, log_var])]
    sub x1 -> x0, other arithmetic: 1.2 us -> none  [local(): var_grad = 1.0 - var_weight * lang_mean]
    slice x0 -> x1, local copies, waits for them, and re-layouts: none -> 1.18 us  [local(): rows[0, 0]]
where the time goes in v3:
time: 89.1 us; the launch traced here: 88.8 us
  Pallas kernels  80.9 us (91%)
  local copies, waits for them, and re-layouts  7.25 us (8%)
    pallas_call x1, Pallas kernels, fused_step(): pl.pallas_call(functools.partial(fused_kernel, n_blk, n_dp, steps), out_s...  80.9 us
    unnamed x3, local copies, waits for them, and re-layouts  4.8 us

profile of v3, /device:TPU:0, one launch (start us, length us, event | category | flops | bytes accessed | tf_op | source)
XLA Modules:
  0.0 88.8 jit_solution(5175007408754325403)
XLA Ops:
  0.6 80.9 %shard_map.127 = (f32[384,256]{1,0:T(8,128)}, f32[128,128]{1,0:T(8,128)}, f32[64,512]{1,0:T(8,128)}, f32[3,128]{1,0:T(4,128)}) custom-call(bf16[1024,1024]{1,0:T(8,128)(2,1)} %bitcast.12, bf16[3072,1024]{1,0:T(8,128)(2,1)} %refs_1_.1, bf16[1024,512]{1,0:T(8,128)(2,1)} %refs_2_.1, bf16[64,512]{1,0:T(8,128)(2,1)} %bitcast.13, s32[1,64]{1,0:T(1,128)} %refs_4_.1, ...), custom_call_target="tpu_custom_call" | custom-call | flops 12884901888 | bytes 10485760 | tf_op jit(solution)/shard_map/pallas_call | solution.py:465
  81.6 1.3 %slice_bitcast_fusion = (f32[100]{0:T(128)}, f32[100]{0:T(128)}) fusion(f32[3,128]{1,0:T(4,128)} %get-tuple-element.10), kind=kLoop, calls=%fused_computation | loop fusion | bytes 1600 | tf_op jit(solution)/shard_map/squeeze | solution.py:531
  82.8 1.2 %slice.9 = f32[1,1]{1,0:T(1,128)} slice(f32[3,128]{1,0:T(4,128)} %get-tuple-element.10), slice={[0:1], [0:1]} | slice | bytes 8 | tf_op jit(solution)/shard_map/slice | solution.py:531
  84.0 1.8 %copy.17 = f32[384,256]{1,0:T(8,128)} copy(f32[384,256]{1,0:T(8,128)} %get-tuple-element.25) | data formatting | bytes 786432
  85.8 1.5 %copy.18 = f32[128,128]{1,0:T(8,128)} copy(f32[128,128]{1,0:T(8,128)} %get-tuple-element.26) | data formatting | bytes 131072
  87.3 1.6 %copy.19 = f32[1,64,512]{2,1,0:T(8,128)} copy(f32[1,64,512]{2,1,0:T(8,128)} %bitcast.11) | data formatting | bytes 262144

commit v4 on v3

--- a/solution.py
+++ b/solution.py
@@ -367,16 +367,17 @@
         ref[...] = (ref[...].astype(F32) + arrived[...].astype(F32)).astype(BF16)
 
     text_copies, total_copies = [], []
-    for t in range(n_z + 3):
+    compute(0, 1 - core)
+    core_copy[0].start()
+    for t in range(n_z + 2):
         if t < n_z:
-            compute(t, 1 - core)
-            core_copy[t].start()
             compute(t, core)
-        if 0 <= t - 1 < n_z:
-            s = t - 1
-            core_copy[s].wait()
-            add(parts.at[s, core], core_in.at[s])
-            first_copy[s].start()
+            if t + 1 < n_z:
+                compute(t + 1, 1 - core)
+                core_copy[t + 1].start()
+            core_copy[t].wait()
+            add(parts.at[t, core], core_in.at[t])
+            first_copy[t].start()
         if t == 1:
             for o in range(1, n_blk):
                 peer = lax.rem(blk + o, n_blk)
@@ -396,14 +397,14 @@
             total_copies = exchange("dp", n_dp, lambda d: total_in.at[d], total_s, total_r)
             for copy in total_copies:
                 copy.start()
-        if 0 <= t - 2 < n_z:
-            s = t - 2
+        if 0 <= t - 1 < n_z:
+            s = t - 1
             first_at, _ = order(s, y, x)
             first_copy[s].wait()
             add(parts.at[s, core, first_at], first_in.at[s])
             second_copy[s].start()
-        if 0 <= t - 3 < n_z:
-            s = t - 3
+        if 0 <= t - 2 < n_z:
+            s = t - 2
             first_at, second_at = order(s, y, x)
             second_copy[s].wait()
             if s < n_z - 1:

time: 89.1 us -> 92.8 us (1.042)
  Pallas kernels: 80.9 us -> 84.6 us
    pallas_call x1, Pallas kernels: 80.9 us -> 84.6 us  [fused_step(): pl.pallas_call(functools.partial(fused_kernel, n_blk, n_dp, steps), out_s...]
where the time goes in v4:
time: 92.8 us; the launch traced here: 92.5 us
  Pallas kernels  84.6 us (91%)
  local copies, waits for them, and re-layouts  7.25 us (8%)
    pallas_call x1, Pallas kernels, fused_step(): pl.pallas_call(functools.partial(fused_kernel, n_blk, n_dp, steps), out_s...  84.6 us
    unnamed x3, local copies, waits for them, and re-layouts  4.8 us

profile of v4, /device:TPU:0, one launch (start us, length us, event | category | flops | bytes accessed | tf_op | source)
XLA Modules:
  0.0 92.5 jit_solution(6147482264339289569)
XLA Ops:
  0.6 84.6 %shard_map.127 = (f32[384,256]{1,0:T(8,128)}, f32[128,128]{1,0:T(8,128)}, f32[64,512]{1,0:T(8,128)}, f32[3,128]{1,0:T(4,128)}) custom-call(bf16[1024,1024]{1,0:T(8,128)(2,1)} %bitcast.12, bf16[3072,1024]{1,0:T(8,128)(2,1)} %refs_1_.1, bf16[1024,512]{1,0:T(8,128)(2,1)} %refs_2_.1, bf16[64,512]{1,0:T(8,128)(2,1)} %bitcast.13, s32[1,64]{1,0:T(1,128)} %refs_4_.1, ...), custom_call_target="tpu_custom_call" | custom-call | flops 12884901888 | bytes 10485760 | tf_op jit(solution)/shard_map/pallas_call | solution.py:466
  85.3 1.3 %slice_bitcast_fusion = (f32[100]{0:T(128)}, f32[100]{0:T(128)}) fusion(f32[3,128]{1,0:T(4,128)} %get-tuple-element.10), kind=kLoop, calls=%fused_computation | loop fusion | bytes 1600 | tf_op jit(solution)/shard_map/squeeze | solution.py:532
  86.5 1.2 %slice.9 = f32[1,1]{1,0:T(1,128)} slice(f32[3,128]{1,0:T(4,128)} %get-tuple-element.10), slice={[0:1], [0:1]} | slice | bytes 8 | tf_op jit(solution)/shard_map/slice | solution.py:532
  87.7 1.8 %copy.17 = f32[384,256]{1,0:T(8,128)} copy(f32[384,256]{1,0:T(8,128)} %get-tuple-element.25) | data formatting | bytes 786432
  89.5 1.5 %copy.18 = f32[128,128]{1,0:T(8,128)} copy(f32[128,128]{1,0:T(8,128)} %get-tuple-element.26) | data formatting | bytes 131072
  91.0 1.6 %copy.19 = f32[1,64,512]{2,1,0:T(8,128)} copy(f32[1,64,512]{2,1,0:T(8,128)} %bitcast.11) | data formatting | bytes 262144
